TPU v7x, 128 devices: a whole 4x4x4 slice. The times are simulated.
128 devices in a mesh: island: 4 (over y_hi, core), fsdp: 32 (over z, y_lo, x).
Axes of the slice: x: 4, y: 4 (y_hi: 2, y_lo: 2; y = y_hi * 2 + y_lo), z: 4, core: 2. Of those that a mesh axis runs over, the one named last changes fastest.
Arguments:
- hidden: bfloat16 [4, 24576, 7168], P('island', 'fsdp'), may hold values from -6 to 6
- grad_out: bfloat16 [4, 24576, 2048], P('island', 'fsdp'), may hold values from -0.076171875 to 0.076171875
- inner_params: float32 [4, 7168, 2048], P('island', 'fsdp'), may hold values from -6 to 6
- first_moment: float32 [4, 7168, 2048], P('island', 'fsdp'), may hold values from -6 to 6
- second_moment: float32 [4, 7168, 2048], P('island', 'fsdp'), may hold values from 0.25 to 16
- anchor: float32 [7168, 2048], P('fsdp', 'island'), may hold values from -6 to 6
- outer_momentum: float32 [7168, 2048], P('fsdp', 'island'), may hold values from -3 to 3
Outputs:
- new_params: bfloat16 [7168, 2048], P('fsdp')
- new_momentum: float32 [7168, 2048], P('fsdp', 'island')
- new_first: float32 [4, 7168, 2048], P('island', 'fsdp')
- new_second: float32 [4, 7168, 2048], P('island', 'fsdp')
All inputs are finite; a program needn't handle non-finite values.
Results may differ from a plain program's by a relative error of at most 0.015.
Values may be sent and summed in bfloat16 or wider, within the bound.
A program may use at most 128 MiB of HBM per device.

v0:
```python
import jax
import jax.numpy as jnp
from jax import lax
from jax.sharding import PartitionSpec as P

INNER_STEP = 20


beta_one = 0.9
beta_two = 0.95
inner_rate = 0.01
decay_rate = 0.1
adam_eps = 1e-08
outer_rate = 0.7
outer_beta = 0.9


def on_device(hidden, grad_out, inner_params, first_moment, second_moment, anchor, outer_momentum):
    local_h = hidden[0]
    local_g = grad_out[0]
    col_quarter = anchor.shape[1]
    full_anchor, full_moment = (
        lax.all_gather(anchor.astype(jnp.bfloat16), "island", axis=1, tiled=True).astype(
            anchor.dtype
        ),
        lax.all_gather(outer_momentum.astype(jnp.bfloat16), "island", axis=1, tiled=True).astype(
            outer_momentum.dtype
        ),
    )
    contract = (((0,), (0,)), ((), ()))
    whole_term = lax.dot_general(local_h, local_g, contract, preferred_element_type=jnp.float32)
    gradient = lax.psum_scatter(
        whole_term.astype(jnp.bfloat16), "fsdp", scatter_dimension=0, tiled=True
    ).astype(jnp.float32)
    corr_one = 1.0 - beta_one**INNER_STEP
    corr_two = 1.0 - beta_two**INNER_STEP
    params_here = inner_params[0]
    first = beta_one * first_moment[0] + (1.0 - beta_one) * gradient
    second = beta_two * second_moment[0] + (1.0 - beta_two) * gradient * gradient
    update = first / corr_one / (jnp.sqrt(second / corr_two) + adam_eps)
    stepped = params_here - inner_rate * (update + decay_rate * params_here)
    island_count = float(lax.axis_size("island"))
    total = lax.psum(stepped.astype(jnp.bfloat16), "island").astype(jnp.float32)
    pseudo = full_anchor - total / island_count
    moment_full = outer_beta * full_moment + pseudo
    new_params = (full_anchor - outer_rate * (pseudo + outer_beta * moment_full)).astype(
        jnp.bfloat16
    )
    offset = lax.axis_index("island") * col_quarter
    new_momentum = lax.dynamic_slice_in_dim(moment_full, offset, col_quarter, 1)
    return (new_params, new_momentum, first[None], second[None])


def solution(mesh):
    placed = (
        P("island", "fsdp", None),
        P("island", "fsdp", None),
        P("island", "fsdp", None),
        P("island", "fsdp", None),
        P("island", "fsdp", None),
        P("fsdp", "island"),
        P("fsdp", "island"),
    )
    return jax.shard_map(
        on_device,
        mesh=mesh,
        in_specs=placed,
        out_specs=(
            P("fsdp", None),
            P("fsdp", "island"),
            P("island", "fsdp", None),
            P("island", "fsdp", None),
        ),
        check_vma=False,
    )
```

profile of v0, /device:TPU:1, one launch (start us, length us, event | category | flops | bytes accessed | tf_op | source)
XLA Modules:
  0.0 426.1 jit_solution(1179652217765693363)
XLA Ops:
  7.2 0.0 copy-start
  7.2 0.0 reduce-scatter.2.cloned.1.call-start
  7.2 1.8 copy-done
  9.1 31.0 %convolution_convert_fusion = bf16[7168,2048]{1,0:T(8,128)(2,1)} fusion(bf16[1,768,7168]{2,1,0:T(8,128)(2,1)} %param.7, bf16[1,768,2048]{2,1,0:T(8,128)(2,1)S(1)} %copy-done), kind=kOutput, calls=%fused_computation | convolution fusion | flops 22563258368 | bytes 43515904 | tf_op jit(solution)/shard_map/dot_general | solution.py:31
  40.0 0.0 reduce-scatter.2.cloned.1.call-update
  40.1 0.0 all-reduce.2.cloned.1.call-start
  40.1 324.4 %reduce-scatter.2.cloned.1.call-done = bf16[224,2048]{1,0:T(8,128)(2,1)} async-done(((bf16[7168,2048]{1,0:T(8,128)(2,1)}), bf16[224,2048]{1,0:T(8,128)(2,1)}) %reduce-scatter.2.cloned.1.call-update) | async-done | bytes 917520 | tf_op jit(solution)/shard_map/reduce_scatter | solution.py:32
  364.6 6.5 %fusion.9 = (f32[1,224,2048]{2,1,0:T(8,128)}, bf16[224,2048]{1,0:T(8,128)(2,1)}, f32[1,224,2048]{2,1,0:T(8,128)}) fusion(bf16[224,2048]{1,0:T(8,128)(2,1)} %reduce-scatter.2.cloned.1.call-done, f32[1,224,2048]{2,1,0:T(8,128)} %param.11, f32[1,224,2048]{2,1,0:T(8,128)} %param.10, f32[1,224,2048]{2,1,0:T(8,128)} %param.9), kind=kLoop, calls=%fused_computation.17 | loop fusion | flops 7798784 | bytes 11010048 | tf_op jit(solution)/shard_map/broadcast_in_dim | solution.py:51
  371.0 0.0 all-reduce.2.cloned.1.call-update
  371.1 1.7 convert_element_type.27
  372.8 1.0 convert_element_type.33
  373.8 17.8 %all_gather.6 = bf16[224,2048]{1,0:T(8,128)(2,1)} all-gather(bf16[224,512]{1,0:T(8,128)(2,1)} %convert_element_type.27), channel_id=1, replica_groups=mesh['island'=4,'fsdp'=32] {'island'}, dimensions={1}, use_global_device_ids=true | all-gather | bytes 1146880 | tf_op jit(solution)/shard_map/all_gather | solution.py:23
  391.6 11.4 %all_gather.7 = bf16[224,2048]{1,0:T(8,128)(2,1)} all-gather(bf16[224,512]{1,0:T(8,128)(2,1)S(1)} %convert_element_type.33), channel_id=1, replica_groups=mesh['island'=4,'fsdp'=32] {'island'}, dimensions={1}, use_global_device_ids=true | all-gather | bytes 1146880 | tf_op jit(solution)/shard_map/all_gather | solution.py:26
  403.0 12.1 %all-reduce.2.cloned.1.call-done = bf16[224,2048]{1,0:T(8,128)(2,1)} async-done(((bf16[224,2048]{1,0:T(8,128)(2,1)}), bf16[224,2048]{1,0:T(8,128)(2,1)}) %all-reduce.2.cloned.1.call-update) | async-done | bytes 917520 | tf_op jit(solution)/shard_map/psum | solution.py:43
  415.1 3.4 multiply_add_fusion
  418.5 0.8 constant_dynamic-slice_fusion
Async XLA Ops:
  7.2 1.9 copy-start
  7.2 357.4 %reduce-scatter.2.cloned.1.call-start = ((), (), s32[]{:S(2)}) async-start(), calls=%async_computation.1 | async-start | bytes 30277632 | tf_op jit(solution)/shard_map/reduce_scatter | solution.py:32
  40.1 375.0 %all-reduce.2.cloned.1.call-start = ((), (), s32[]{:S(2)}) async-start(), calls=%async_computation.2 | async-start | bytes 1835008 | tf_op jit(solution)/shard_map/psum | solution.py:43
Sparse Core Ops, SparseCore 0:
  40.2 324.3 reduce-scatter.1
  371.2 43.9 all-reduce.1
where the time goes:
time: 426 us
  waiting for transfers between devices  337 us (79%)
  matrix products  31 us (7%)
  blocking collectives  29.2 us (7%)
  between operations  14.1 us (3%)
  other arithmetic  12.6 us (3%)
    reduce_scatter x1, waiting for transfers between devices, on_device(): lax.psum_scatter(whole_term.astype(jnp.bfloat16), 'fsdp', scatter_dimensi...  324 us
    dot_general x1, matrix products, on_device(): lax.dot_general(local_h, local_g, contract, preferred_element_type=jnp.fl...  31 us
    all_gather x1, blocking collectives, on_device(): lax.all_gather(anchor.astype(jnp.bfloat16), 'island', axis=1, tiled=True)  17.8 us
    psum x1, waiting for transfers between devices, on_device(): total = lax.psum(stepped.astype(jnp.bfloat16), 'island').astype(jnp.float32)  12.1 us
    all_gather x1, blocking collectives, on_device(): lax.all_gather(outer_momentum.astype(jnp.bfloat16), 'island', axis=1, til...  11.4 us
  transfers between devices with their start and end apart: 2, of which 2 were waited for; matrix products, arithmetic and copies ran while one was open for 1% of the time, Pallas kernels for 0%

commit v1 on v0

v1 whole, which is shorter than its diff:
```python
import functools

import jax
import jax.numpy as jnp
from jax import lax
from jax.experimental import pallas as pl
from jax.experimental.pallas import tpu as pltpu
from jax.sharding import PartitionSpec as P

INNER_STEP = 20
beta_one = 0.9
beta_two = 0.95
inner_rate = 0.01
decay_rate = 0.1
adam_eps = 1e-08
outer_rate = 0.7
outer_beta = 0.9

MESH = pl.DeviceIdType.MESH
TOK, FF, D = 768, 7168, 2048
ROWS, HALF = 224, 112
QROWS = 4 * ROWS
WIDE = 256
GROUPS = 4
STEPS = 8 * GROUPS
SLOTS = 16
D1, D2, D3, D4, D5 = 2, 4, 6, 8, 11
F32, BF16 = jnp.float32, jnp.bfloat16


ROWS_Y = 32
LATE = ROWS - ROWS_Y


def offset_of(q):
    return jnp.where(q == 2, 3, jnp.where(q == 3, 0, 2 - q))


def kernel(
    hid, gra, par_h, mom_h, var_h, anc_h, out_h,
    o_par, o_mom, o_first, o_second,
    hch, hT, G, par, mom, var, anc, om,
    ring, ey, sy, c1, tb, tf, st, nbuf,
    rA, rYE, rY, rC, rE,
    ld, hs, sA, sYE, sY, sC, sE, sN, outs, loc,
    qA, qYE, qY, qC, qE, qN,
):
    isl, f = lax.axis_index("island"), lax.axis_index("fsdp")
    yh, co = isl // 2, isl % 2
    z, y, x = f // 8, (f // 4) % 2, f % 4
    other_y = 1 - y

    def fs(zz, yy, xx):
        return zz * 8 + yy * 4 + xx

    xr, xl = (isl, fs(z, y, (x + 1) % 4)), (isl, fs(z, y, (x + 3) % 4))
    zr, zl = (isl, fs((z + 1) % 4, y, x)), (isl, fs((z + 3) % 4, y, x))
    ynb = (isl, fs(z, other_y, x))
    A = ((xr, xl), (zr, zl))
    C = ((zr, zl), (xr, xl))
    a_of = (x, z)
    c_of = (z, x)

    def block(k, a, yy, c):
        return fs(c, yy, a) if k == 0 else fs(a, yy, c)

    def chunk_q(n):
        yy = jnp.where(n < 4, other_y, y)
        return ((z + offset_of(n % 4)) % 4) * 2 + yy

    def chunk_load(n):
        return pltpu.make_async_copy(
            hid.at[0, :, pl.ds(pl.multiple_of(chunk_q(n) * QROWS, 128), QROWS)],
            hch.at[n % 2],
            hs.at[n % 2],
        )

    gload = pltpu.make_async_copy(gra.at[0], G, ld.at[0])
    rest = [
        pltpu.make_async_copy(src, dst, ld.at[1 + n])
        for n, (src, dst) in enumerate(
            ((par_h.at[0], par), (mom_h.at[0], mom), (var_h.at[0], var), (anc_h, anc), (out_h, om))
        )
    ]
    chunk_load(0).start()
    gload.start()
    chunk_load(1).start()

    bar = pltpu.get_barrier_semaphore()
    peers = [xr, xl, zr, zl, ynb, (yh * 2 + 1 - co, f), ((1 - yh) * 2, f), ((1 - yh) * 2 + 1, f)]
    for peer in peers:
        pl.semaphore_signal(bar, inc=1, device_id=peer, device_id_type=MESH)

    def remote(src, dst, ss, rs, dev):
        return pltpu.make_async_remote_copy(
            src_ref=src, dst_ref=dst, send_sem=ss, recv_sem=rs, device_id=dev, device_id_type=MESH
        )

    parts = {True: (pl.ds(ROWS_Y, LATE // 2), pl.ds(ROWS_Y + LATE // 2, LATE // 2)), False: (pl.ds(0, HALF), pl.ds(HALF, HALF))}
    used = {True: pl.ds(0, LATE // 2), False: pl.ds(0, HALF)}

    def ring_send(k, p, s, d, kind, oth):
        tile = 0 if kind == 0 else 1 + d
        rows = parts[oth][1 - d if kind == 1 else d]
        return remote(
            ring.at[k, p, tile, rows], rA.at[k, s, d, kind, used[oth]], sA.at[k, p, d, kind], qA.at[k, s, d, kind], A[k][d]
        )

    def yearly(k, g, p):
        return remote(ey.at[k, p], rYE.at[k, g, p], sYE.at[k, p], qYE.at[k, g, p], ynb)

    def ysend(k, g, p):
        return remote(sy.at[k, p], rY.at[k, g, p], sY.at[k, p], qY.at[k, g, p], ynb)

    def csend(k, g, d, kind):
        rows = parts[False][1 - d if kind == 1 else d]
        src = c1.at[k, rows] if kind == 0 else tb.at[k, d, rows]
        return remote(src, rC.at[k, g, d, kind], sC.at[k, d, kind], qC.at[k, g, d, kind], C[k][d])

    def columns(k, g, b):
        return pl.ds(pl.multiple_of(1024 * k + 512 * b + 128 * g, 128), 128)

    def esend(k, g, b, slot, dev):
        return remote(st.at[k, b], rE.at[g, slot], sE.at[k, b], qE.at[g, slot], dev)

    def nsend(g, n, dev):
        cols = pl.ds(pl.multiple_of(512 * isl + 128 * g, 128), 128)
        return remote(nbuf.at[g], o_par.at[:, cols], sN.at[g, n], qN.at[isl, g], dev)

    def transpose_chunk(n):
        chunk_load(n).wait()
        base = chunk_q(n) * QROWS
        for j in range(QROWS // 128):
            rows = pl.ds(pl.multiple_of(base + 128 * j, 128), 128)
            hT[rows, :] = hch[n % 2, :, pl.ds(128 * j, 128)].T

        if isinstance(n, int):
            chunk_load(n + 2).start()
        else:

            @pl.when(n + 2 < 8)
            def _():
                chunk_load(n + 2).start()

    def by_y(p, body):
        @pl.when(p < 4)
        def _():
            body(True)

        @pl.when(p >= 4)
        def _():
            body(False)

    def stage0(k, t, before=None):
        g, p, s = t // 8, t % 8, t % SLOTS
        yy = jnp.where(p < 4, other_y, y)
        cc = (c_of[k] + offset_of(p % 4)) % 4

        @pl.when(g >= 1)
        def _():
            def free(oth):
                for d in range(2):
                    for kind in range(3):
                        ring_send(k, p, 0, d, kind, oth).wait_send()
                if oth:
                    yearly(k, g, p).wait_send()

            by_y(p, free)

        @pl.when(p >= 4)
        def _():
            yearly(k, g, p - 4).wait_recv()

        rhs = jnp.concatenate([G[:, columns(k, g, 0)], G[:, columns(k, g, 1)]], axis=1)
        for j, off in enumerate((2, 1, 3, 0)):
            if before is not None:
                before(j)
            r = block(k, (a_of[k] + off) % 4, yy, cc)
            lhs = hT[pl.ds(pl.multiple_of(r * ROWS, 32), ROWS), :]
            tile = jnp.dot(lhs, rhs, preferred_element_type=F32).astype(BF16)
            ring[k, p, j] = tile

            def finish(oth, j=j, tile=tile):
                if oth:
                    ey[k, p, j] = tile[:ROWS_Y]
                else:
                    ring[k, p, j, pl.ds(0, ROWS_Y)] = tile[:ROWS_Y] + rYE[k, g, p - 4, j]
                if j == 0:
                    for d in range(2):
                        ring_send(k, p, s, d, 0, oth).start()
                elif j < 3:
                    ring_send(k, p, s, j - 1, 1, oth).start()
                elif oth:
                    yearly(k, g, p).start()

            by_y(p, finish)

    def stage1(k, t):
        g, p, s = t // 8, t % 8, t % SLOTS

        def body(oth):
            for d in range(2):
                rows = parts[oth][d]
                ring_send(k, p, s, d, 0, oth).wait_recv()
                ring[k, p, 1 + d, rows] = ring[k, p, 1 + d, rows] + rA[k, s, d, 0, used[oth]]
                ring_send(k, p, s, d, 2, oth).start()

        by_y(p, body)

    def stage2(k, t):
        g, p, s = t // 8, t % 8, t % SLOTS

        def body(oth):
            for d in range(2):
                for kind in (1, 2):
                    ring_send(k, p, s, d, kind, oth).wait_recv()

            def total(q):
                return (
                    ring[k, p, 3, parts[oth][q]].astype(F32)
                    + rA[k, s, 0, 2 - q, used[oth]].astype(F32)
                    + rA[k, s, 1, 1 + q, used[oth]].astype(F32)
                )

            if oth:

                @pl.when(g >= 1)
                def _():
                    ysend(k, g, p).wait_send()

                for q in range(2):
                    sy[k, p, pl.ds(q * LATE // 2, LATE // 2)] = total(q).astype(BF16)
                ysend(k, g, p).start()
                return

            for q in range(2):
                tf[k, parts[False][q]] = total(q)
            ysend(k, g, p - 4).wait_recv()
            late = pl.ds(ROWS_Y, LATE)
            tf[k, late] = tf[k, late] + rY[k, g, p - 4].astype(F32)

            @pl.when(p == 4)
            def _():
                @pl.when(g >= 1)
                def _():
                    for d in range(2):
                        csend(k, g, d, 0).wait_send()

                c1[k] = tf[k].astype(BF16)
                for d in range(2):
                    csend(k, g, d, 0).start()

            for d in range(2):

                @pl.when(p == 5 + d)
                def _(d=d):
                    @pl.when(g >= 1)
                    def _():
                        for kind in (1, 2):
                            csend(k, g, d, kind).wait_send()

                    tb[k, d] = tf[k].astype(BF16)
                    csend(k, g, d, 1).start()

        by_y(p, body)

    def stage3(k, t):
        g, p = t // 8, t % 8
        for d in range(2):

            @pl.when(p == 5 + d)
            def _(d=d):
                rows = parts[False][d]
                csend(k, g, d, 0).wait_recv()
                tb[k, d, rows] = tb[k, d, rows] + rC[k, g, d, 0]
                csend(k, g, d, 2).start()

    corr_one = 1.0 - beta_one**INNER_STEP
    corr_two = 1.0 - beta_two**INNER_STEP

    def stage4(k, t):
        g, p = t // 8, t % 8

        @pl.when(p == 7)
        def _():
            @pl.when(g == 0)
            def _():
                if k == 0:
                    for copy in rest:
                        copy.wait()

            for d in range(2):
                for kind in (1, 2):
                    csend(k, g, d, kind).wait_recv()

            @pl.when(g >= 1)
            def _():
                @pl.when(yh == k)
                def _():
                    for b in range(2):

                        @pl.when(co != b)
                        def _(b=b):
                            esend(k, g, b, 0, (2 * k + b, f)).wait_send()

                @pl.when(yh != k)
                def _():
                    for b in range(2):
                        esend(k, g, b, 1 + co, (2 * k + b, f)).wait_send()

            for b in range(2):
                cols = columns(k, g, b)

                lanes = pl.ds(128 * b, 128)
                for q in range(2):
                    rows = parts[False][q]
                    grad = (
                        tf[k, rows, lanes]
                        + rC[k, g, 0, 2 - q, :, lanes].astype(F32)
                        + rC[k, g, 1, 1 + q, :, lanes].astype(F32)
                    )
                    here = par[rows, cols]
                    first = beta_one * mom[rows, cols] + (1.0 - beta_one) * grad
                    second = beta_two * var[rows, cols] + (1.0 - beta_two) * grad * grad
                    mom[rows, cols] = first
                    var[rows, cols] = second
                    update = first / corr_one / (jnp.sqrt(second / corr_two) + adam_eps)
                    stepped = here - inner_rate * (update + decay_rate * here)
                    st[k, b, rows] = stepped.astype(BF16)
                    par[rows, cols] = stepped

                @pl.when(jnp.logical_and(yh == k, co != b))
                def _(b=b):
                    esend(k, g, b, 0, (2 * k + b, f)).start()

                @pl.when(yh != k)
                def _(b=b):
                    esend(k, g, b, 1 + co, (2 * k + b, f)).start()

                pltpu.make_async_copy(mom.at[:, cols], o_first.at[0, :, cols], outs.at[0]).start()
                pltpu.make_async_copy(var.at[:, cols], o_second.at[0, :, cols], outs.at[1]).start()

    def others(k):
        return [(2 * k + 1 - co, f), (2 * (1 - k), f), (2 * (1 - k) + 1, f)]

    def stage5(k, t):
        g, p = t // 8, t % 8

        @pl.when(jnp.logical_and(p == 7, yh == k))
        def _():
            for slot in range(3):
                esend(k, g, 0, slot, (2 * k, f)).wait_recv()
            cols = pl.ds(pl.multiple_of(1024 * k + 512 * co + 128 * g, 128), 128)
            local = pl.ds(pl.multiple_of(128 * g, 128), 128)

            for rows in parts[False]:
                total = par[rows, cols]
                for slot in range(3):
                    total = total + rE[g, slot, rows].astype(F32)
                here = anc[rows, local]
                pseudo = here - total / 4.0
                moved = outer_beta * om[rows, local] + pseudo
                om[rows, local] = moved
                nbuf[g, rows] = (here - outer_rate * (pseudo + outer_beta * moved)).astype(BF16)
            for n, dev in enumerate(others(k)):
                nsend(g, n, dev).start()
            pltpu.make_async_copy(nbuf.at[g], o_par.at[:, cols], loc.at[g]).start()
            pltpu.make_async_copy(om.at[:, local], o_mom.at[:, local], outs.at[2]).start()

    def step(t, _):
        @pl.when(jnp.logical_and(t >= 1, t < 5))
        def _():
            transpose_chunk(t + 3)

        @pl.when(t == 8)
        def _():
            for copy in rest:
                copy.start()

        for delay, stage in ((0, stage0), (D1, stage1), (D2, stage2), (D3, stage3), (D4, stage4), (D5, stage5)):
            for k in range(2):
                tau = t - delay

                @pl.when(jnp.logical_and(tau >= 0, tau < STEPS))
                def _(tau=tau, k=k, stage=stage):
                    stage(k, tau)

        return 0

    transpose_chunk(0)
    gload.wait()
    pl.semaphore_wait(bar, len(peers))
    stage0(0, jnp.int32(0))

    def before(j):
        if j >= 1:
            transpose_chunk(j)

    stage0(1, jnp.int32(0), before)
    lax.fori_loop(1, STEPS + D5, step, 0)

    for k in range(2):
        for p in range(8):
            for d in range(2):
                for kind in range(3):
                    ring_send(k, p, 0, d, kind, p < 4).wait_send()
        for p in range(4):
            yearly(k, 0, p).wait_send()
            ysend(k, 0, p).wait_send()
        for d in range(2):
            for kind in range(3):
                csend(k, 0, d, kind).wait_send()
        for b in range(2):

            @pl.when(jnp.logical_or(yh != k, co != b))
            def _(k=k, b=b):
                esend(k, 0, b, 0, (2 * k + b, f)).wait_send()

    pltpu.make_async_copy(mom.at[:, pl.ds(0, D * GROUPS // 4)], o_first.at[0, :, pl.ds(0, D * GROUPS // 4)], outs.at[0]).wait()
    pltpu.make_async_copy(var.at[:, pl.ds(0, D * GROUPS // 4)], o_second.at[0, :, pl.ds(0, D * GROUPS // 4)], outs.at[1]).wait()
    pltpu.make_async_copy(om.at[:, pl.ds(0, 128 * GROUPS)], o_mom.at[:, pl.ds(0, 128 * GROUPS)], outs.at[2]).wait()
    for g in range(GROUPS):
        for k in range(2):

            @pl.when(yh == k)
            def _(k=k, g=g):
                for n, dev in enumerate(others(k)):
                    nsend(g, n, dev).wait_send()

        pltpu.make_async_copy(nbuf.at[g], o_par.at[:, pl.ds(0, 128)], loc.at[g]).wait()
        for i in range(4):

            @pl.when(isl != i)
            def _(i=i, g=g):
                cols = pl.ds(512 * i + 128 * g, 128)
                remote(nbuf.at[g], o_par.at[:, cols], sN.at[g, 0], qN.at[i, g], ynb).wait_recv()


PIECES = 2


def hand_on(*refs):
    sources, targets, held, sems = refs[:4], refs[4:8], refs[8:12], refs[12]
    rows = ROWS // PIECES
    pairs = []
    for n, (src, dst, mid) in enumerate(zip(sources, targets, held)):
        for m in range(PIECES):
            part = (slice(None),) * (len(src.shape) - 2) + (pl.ds(m * rows, rows),)
            pairs.append(
                (
                    pltpu.make_async_copy(src.at[part], mid.at[part], sems.at[0, n, m]),
                    pltpu.make_async_copy(mid.at[part], dst.at[part], sems.at[1, n, m]),
                )
            )
    for load, _ in pairs:
        load.start()
    for load, store in pairs:
        load.wait()
        store.start()
    for _, store in pairs:
        store.wait()


def on_device(hidden, grad_out, inner_params, first_moment, second_moment, anchor, outer_momentum):
    dma = pltpu.SemaphoreType.DMA
    vm = pltpu.VMEM
    tile, half, narrow = (ROWS, WIDE), (HALF, WIDE), (ROWS, 128)
    any_spec = pl.BlockSpec(memory_space=pl.ANY)
    shapes = (
        jax.ShapeDtypeStruct((ROWS, D), BF16),
        jax.ShapeDtypeStruct((ROWS, 512), F32),
        jax.ShapeDtypeStruct((1, ROWS, D), F32),
        jax.ShapeDtypeStruct((1, ROWS, D), F32),
    )
    results = pl.pallas_call(
        kernel,
        name="window",
        out_shape=shapes,
        in_specs=[any_spec] * 7,
        out_specs=(any_spec,) * 4,
        scratch_shapes=[
            vm((2, TOK, QROWS), BF16),
            vm((FF, TOK), BF16),
            vm((TOK, D), BF16),
            vm((ROWS, D), F32),
            vm((ROWS, D), F32),
            vm((ROWS, D), F32),
            vm((ROWS, 512), F32),
            vm((ROWS, 512), F32),
            vm((2, 8, 4) + tile, BF16),
            vm((2, 4, 4, ROWS_Y, WIDE), BF16),
            vm((2, 4, LATE, WIDE), BF16),
            vm((2,) + tile, BF16),
            vm((2, 2) + tile, BF16),
            vm((2,) + tile, F32),
            vm((2, 2) + narrow, BF16),
            vm((GROUPS,) + narrow, BF16),
            vm((2, SLOTS, 2, 3) + half, BF16),
            vm((2, GROUPS, 4, 4, ROWS_Y, WIDE), BF16),
            vm((2, GROUPS, 4, LATE, WIDE), BF16),
            vm((2, GROUPS, 2, 3) + half, BF16),
            vm((GROUPS, 3) + narrow, BF16),
            dma((6,)),
            dma((2,)),
            dma((2, 8, 2, 3)),
            dma((2, 4)),
            dma((2, 4)),
            dma((2, 2, 3)),
            dma((2, 2)),
            dma((GROUPS, 3)),
            dma((3,)),
            dma((GROUPS,)),
            dma((2, SLOTS, 2, 3)),
            dma((2, GROUPS, 4)),
            dma((2, GROUPS, 4)),
            dma((2, GROUPS, 2, 3)),
            dma((GROUPS, 3)),
            dma((4, GROUPS)),
        ],
        compiler_params=pltpu.CompilerParams(
            collective_id=0, has_side_effects=True, vmem_limit_bytes=60 * 1024 * 1024
        ),
        cost_estimate=pl.CostEstimate(flops=2 * TOK * FF * D, bytes_accessed=32 << 20, transcendentals=0),
    )(hidden, grad_out, inner_params, first_moment, second_moment, anchor, outer_momentum)
    return pl.pallas_call(
        hand_on,
        name="hand_on",
        out_shape=shapes,
        in_specs=[any_spec] * 4,
        out_specs=(any_spec,) * 4,
        scratch_shapes=[vm(shape.shape, shape.dtype) for shape in shapes] + [dma((2, 4, PIECES))],
    )(*results)


def solution(mesh):
    placed = (
        P("island", "fsdp", None),
        P("island", "fsdp", None),
        P("island", "fsdp", None),
        P("island", "fsdp", None),
        P("island", "fsdp", None),
        P("fsdp", "island"),
        P("fsdp", "island"),
    )
    return jax.shard_map(
        on_device,
        mesh=mesh,
        in_specs=placed,
        out_specs=(
            P("fsdp", None),
            P("fsdp", "island"),
            P("island", "fsdp", None),
            P("island", "fsdp", None),
        ),
        check_vma=False,
    )
```

time: 426 us -> 164 us (0.38)
  waiting for transfers between devices: 337 us -> 0 us
  Pallas kernels: 0 us -> 163 us
  matrix products: 31 us -> 0 us
  blocking collectives: 29.2 us -> 0 us
  between operations: 14.1 us -> 0.64 us
  other arithmetic: 12.6 us -> 0 us
    reduce_scatter x1 -> x0, waiting for transfers between devices: 324 us -> none  [on_device(): lax.psum_scatter(whole_term.astype(jnp.bfloat16), 'fsdp', scatter_dimensi...]
    pallas_call x0 -> x2, Pallas kernels: none -> 163 us  [the longest x1 159 us: on_device(): pl.pallas_call(kernel, name='window', out_shape=shapes, in_specs=[any_spe...]
    dot_general x1 -> x0, matrix products: 31 us -> none  [on_device(): lax.dot_general(local_h, local_g, contract, preferred_element_type=jnp.fl...]
    all_gather x2 -> x0, blocking collectives: 29.2 us -> none  [the longest x1 17.8 us: on_device(): lax.all_gather(anchor.astype(jnp.bfloat16), 'island', axis=1, tiled=True)]
    psum x1 -> x0, waiting for transfers between devices: 12.1 us -> none  [on_device(): total = lax.psum(stepped.astype(jnp.bfloat16), 'island').astype(jnp.float32)]
    broadcast_in_dim x1 -> x0, other arithmetic: 6.47 us -> none  [on_device(): return (new_params, new_momentum, first[None], second[None])]
  transfers between devices with their start and end apart: 2 -> 0, of which waited for: 2 -> 0; matrix products, arithmetic and copies ran while one was open for 1% -> 0% of each run, Pallas kernels for 0% -> 0%
where the time goes in v1:
time: 164 us
  Pallas kernels  163 us (99%)
    pallas_call x1, Pallas kernels, on_device(): pl.pallas_call(kernel, name='window', out_shape=shapes, in_specs=[any_spe...  159 us
    pallas_call x1, Pallas kernels, on_device(): pl.pallas_call(hand_on, name='hand_on', out_shape=shapes, in_specs=[any_s...  4.65 us

profile of v1, /device:TPU:1, one launch (start us, length us, event | category | flops | bytes accessed | tf_op | source)
XLA Modules:
  0.0 164.1 jit_solution(13614761552565940553)
XLA Ops:
  0.6 158.8 %window.1 = (bf16[224,2048]{1,0:T(8,128)(2,1)}, f32[224,512]{1,0:T(8,128)}, f32[1,224,2048]{2,1,0:T(8,128)}, f32[1,224,2048]{2,1,0:T(8,128)}) custom-call(bf16[1,768,7168]{2,1,0:T(8,128)(2,1)} %hid.1, bf16[1,768,2048]{2,1,0:T(8,128)(2,1)} %gra.1, f32[1,224,2048]{2,1,0:T(8,128)} %par_h.1, f32[1,224,2048]{2,1,0:T(8,128)} %mom_h.1, f32[1,224,2048]{2,1,0:T(8,128)} %var_h.1, ...), custom_call_target="tpu_custom_call" | custom-call | flops 22548578304 | bytes 33554432 | tf_op jit(solution)/shard_map/window/pallas_call | solution.py:475
  159.4 4.7 %hand_on.1 = (bf16[224,2048]{1,0:T(8,128)(2,1)}, f32[224,512]{1,0:T(8,128)}, f32[1,224,2048]{2,1,0:T(8,128)}, f32[1,224,2048]{2,1,0:T(8,128)}) custom-call(bf16[224,2048]{1,0:T(8,128)(2,1)} %get-tuple-element.8.refs_0_, f32[224,512]{1,0:T(8,128)} %get-tuple-element.9.refs_1_, f32[1,224,2048]{2,1,0:T(8,128)} %get-tuple-element.10.refs_2_, ...), custom_call_target="tpu_custom_call" | custom-call | tf_op jit(solution)/shard_map/hand_on/pallas_call | solution.py:525

commit v2 on v1

v2 whole, which is shorter than its diff:
```python
import functools

import jax
import jax.numpy as jnp
from jax import lax
from jax.experimental import pallas as pl
from jax.experimental.pallas import tpu as pltpu
from jax.sharding import PartitionSpec as P

INNER_STEP = 20
beta_one = 0.9
beta_two = 0.95
inner_rate = 0.01
decay_rate = 0.1
adam_eps = 1e-08
outer_rate = 0.7
outer_beta = 0.9

MESH = pl.DeviceIdType.MESH
TOK, FF, D = 768, 7168, 2048
ROWS, HALF = 224, 112
QROWS = 4 * ROWS
WIDE = 256
GROUPS = 4
STEPS = 8 * GROUPS
SLOTS = 16
D1, D2, D3, D4, D5, D6, D7 = 2, 4, 6, 8, 9, 12, 15
F32, BF16 = jnp.float32, jnp.bfloat16


EARLY = (32, 32)


def offset_of(q):
    return jnp.where(q == 2, 3, jnp.where(q == 3, 0, 2 - q))


def kernel(
    hid, gra, par_h, mom_h, var_h, anc_h, out_h,
    o_par, om, mom, var,
    hch, hT, G, par, anc,
    ring, ey, sy, c1, tb, tf, st, ps, nbuf,
    rA, rYE, rY, rC, rE,
    ld, hs, sA, sYE, sY, sC, sE, sP, sN, sR,
    qA, qYE, qY, qC, qE, qN,
):
    isl, f = lax.axis_index("island"), lax.axis_index("fsdp")
    yh, co = isl // 2, isl % 2
    z, y, x = f // 8, (f // 4) % 2, f % 4
    other_y = 1 - y

    def fs(zz, yy, xx):
        return zz * 8 + yy * 4 + xx

    xr, xl = (isl, fs(z, y, (x + 1) % 4)), (isl, fs(z, y, (x + 3) % 4))
    zr, zl = (isl, fs((z + 1) % 4, y, x)), (isl, fs((z + 3) % 4, y, x))
    ynb = (isl, fs(z, other_y, x))
    A = ((xr, xl), (zr, zl))
    C = ((zr, zl), (xr, xl))
    a_of = (x, z)
    c_of = (z, x)

    def block(k, a, yy, c):
        return fs(c, yy, a) if k == 0 else fs(a, yy, c)

    def chunk_q(n):
        yy = jnp.where(n < 4, other_y, y)
        return ((z + offset_of(n % 4)) % 4) * 2 + yy

    def chunk_load(n):
        return pltpu.make_async_copy(
            hid.at[0, :, pl.ds(pl.multiple_of(chunk_q(n) * QROWS, 128), QROWS)],
            hch.at[n % 2],
            hs.at[n % 2],
        )

    gload = pltpu.make_async_copy(gra.at[0], G, ld.at[0])
    rest = [
        pltpu.make_async_copy(src, dst, ld.at[1 + n])
        for n, (src, dst) in enumerate(
            ((par_h.at[0], par), (mom_h.at[0], mom), (var_h.at[0], var), (anc_h, anc), (out_h, om))
        )
    ]
    chunk_load(0).start()
    gload.start()
    chunk_load(1).start()

    bar = pltpu.get_barrier_semaphore()
    partner, far = (yh * 2 + 1 - co, f), ((1 - yh) * 2 + co, f)
    peers = [xr, xl, zr, zl, ynb, partner, far]
    for peer in peers:
        pl.semaphore_signal(bar, inc=1, device_id=peer, device_id_type=MESH)

    def remote(src, dst, ss, rs, dev):
        return pltpu.make_async_remote_copy(
            src_ref=src, dst_ref=dst, send_sem=ss, recv_sem=rs, device_id=dev, device_id_type=MESH
        )

    def parts(piece):
        oth, early = piece
        if not oth:
            return ((0, HALF), (HALF, HALF))
        size = -(-(ROWS - early) // 32) * 16
        return ((early, size), (early + size, ROWS - early - size))

    def ring_send(k, p, s, d, kind, piece):
        tile = 0 if kind == 0 else 1 + d
        start, size = parts(piece)[1 - d if kind == 1 else d]
        return remote(
            ring.at[k, p, tile, pl.ds(start, size)],
            rA.at[k, s, d, kind, pl.ds(0, size)],
            sA.at[k, p, d, kind],
            qA.at[k, s, d, kind],
            A[k][d],
        )

    def yearly(k, g, p, early):
        rows = pl.ds(0, early)
        return remote(ey.at[k, p, :, rows], rYE.at[k, g, p, :, rows], sYE.at[k, p], qYE.at[k, g, p], ynb)

    def ysend(k, g, p, early):
        rows = pl.ds(0, ROWS - early)
        return remote(sy.at[k, p, rows], rY.at[k, g, p, rows], sY.at[k, p], qY.at[k, g, p], ynb)

    halves = (pl.ds(0, HALF), pl.ds(HALF, HALF))

    def csend(k, g, d, kind):
        rows = halves[1 - d if kind == 1 else d]
        src = c1.at[k, rows] if kind == 0 else tb.at[k, d, rows]
        return remote(src, rC.at[k, g, d, kind], sC.at[k, d, kind], qC.at[k, g, d, kind], C[k][d])

    def columns(k, g, b):
        return pl.ds(pl.multiple_of(1024 * k + 512 * b + 128 * g, 128), 128)

    def esend(k, g):
        return remote(st.at[k, 1 - co], rE.at[k, g, 0], sE.at[k], qE.at[k, g, 0], partner)

    def psend(k, g):
        return remote(ps, rE.at[k, g, 1], sP, qE.at[k, g, 1], far)

    def param_columns(island, g):
        return pl.ds(pl.multiple_of(512 * island + 128 * g, 128), 128)

    def nsend(g, n):
        return remote(nbuf.at[g], o_par.at[:, param_columns(isl, g)], sN.at[g, n], qN.at[isl, g], (partner, far)[n])

    def relay(g):
        owner = 2 * (1 - yh) + co
        here = o_par.at[:, param_columns(owner, g)]
        return remote(here, here, sR.at[g], qN.at[owner, g], partner)

    def transpose_chunk(n):
        chunk_load(n).wait()
        base = chunk_q(n) * QROWS
        for j in range(QROWS // 128):
            rows = pl.ds(pl.multiple_of(base + 128 * j, 128), 128)
            hT[rows, :] = hch[n % 2, :, pl.ds(128 * j, 128)].T

        if isinstance(n, int):
            chunk_load(n + 2).start()
        else:

            @pl.when(n + 2 < 8)
            def _():
                chunk_load(n + 2).start()

    def by_piece(p, body):
        for n, piece in enumerate(((True, EARLY[0]), (True, EARLY[1]), (False, EARLY[0]), (False, EARLY[1]))):

            @pl.when(p // 2 == n)
            def _(piece=piece):
                body(piece)

    def stage0(k, t, before=None):
        g, p, s = t // 8, t % 8, t % SLOTS
        yy = jnp.where(p < 4, other_y, y)
        cc = (c_of[k] + offset_of(p % 4)) % 4

        @pl.when(g >= 1)
        def _():
            def free(piece):
                for d in range(2):
                    for kind in range(3):
                        ring_send(k, p, 0, d, kind, piece).wait_send()
                if piece[0]:
                    yearly(k, g, p, piece[1]).wait_send()

            by_piece(p, free)

        def arrived(piece):
            if not piece[0]:
                yearly(k, g, p - 4, piece[1]).wait_recv()

        by_piece(p, arrived)

        rhs = jnp.concatenate([G[:, columns(k, g, 0)], G[:, columns(k, g, 1)]], axis=1)
        for j, off in enumerate((2, 1, 3, 0)):
            if before is not None:
                before(j)
            r = block(k, (a_of[k] + off) % 4, yy, cc)
            lhs = hT[pl.ds(pl.multiple_of(r * ROWS, 32), ROWS), :]
            tile = jnp.dot(lhs, rhs, preferred_element_type=F32).astype(BF16)
            ring[k, p, j] = tile

            def finish(piece, j=j, tile=tile):
                oth, early = piece
                if oth:
                    ey[k, p, j, pl.ds(0, early)] = tile[:early]
                else:
                    ring[k, p, j, pl.ds(0, early)] = tile[:early] + rYE[k, g, p - 4, j, pl.ds(0, early)]
                if j == 0:
                    for d in range(2):
                        ring_send(k, p, s, d, 0, piece).start()
                elif j < 3:
                    ring_send(k, p, s, j - 1, 1, piece).start()
                elif oth:
                    yearly(k, g, p, early).start()

            by_piece(p, finish)

    def stage1(k, t):
        g, p, s = t // 8, t % 8, t % SLOTS

        def body(piece):
            for d in range(2):
                start, size = parts(piece)[d]
                rows = pl.ds(start, size)
                ring_send(k, p, s, d, 0, piece).wait_recv()
                ring[k, p, 1 + d, rows] = ring[k, p, 1 + d, rows] + rA[k, s, d, 0, pl.ds(0, size)]
                ring_send(k, p, s, d, 2, piece).start()

        by_piece(p, body)

    def stage2(k, t):
        g, p, s = t // 8, t % 8, t % SLOTS

        def body(piece):
            oth, early = piece
            for d in range(2):
                for kind in (1, 2):
                    ring_send(k, p, s, d, kind, piece).wait_recv()

            def total(q):
                start, size = parts(piece)[q]
                return (
                    ring[k, p, 3, pl.ds(start, size)].astype(F32)
                    + rA[k, s, 0, 2 - q, pl.ds(0, size)].astype(F32)
                    + rA[k, s, 1, 1 + q, pl.ds(0, size)].astype(F32)
                )

            if oth:

                @pl.when(g >= 1)
                def _():
                    ysend(k, g, p, early).wait_send()

                for q in range(2):
                    start, size = parts(piece)[q]
                    sy[k, p, pl.ds(start - early, size)] = total(q).astype(BF16)
                ysend(k, g, p, early).start()
                return

            for q in range(2):
                tf[k, halves[q]] = total(q)
            ysend(k, g, p - 4, early).wait_recv()
            late = pl.ds(early, ROWS - early)
            tf[k, late] = tf[k, late] + rY[k, g, p - 4, pl.ds(0, ROWS - early)].astype(F32)

            @pl.when(p == 4)
            def _():
                @pl.when(g >= 1)
                def _():
                    for d in range(2):
                        csend(k, g, d, 0).wait_send()

                c1[k] = tf[k].astype(BF16)
                for d in range(2):
                    csend(k, g, d, 0).start()

            for d in range(2):

                @pl.when(p == 5 + d)
                def _(d=d):
                    @pl.when(g >= 1)
                    def _():
                        for kind in (1, 2):
                            csend(k, g, d, kind).wait_send()

                    tb[k, d] = tf[k].astype(BF16)
                    csend(k, g, d, 1).start()

        by_piece(p, body)

    def stage3(k, t):
        g, p = t // 8, t % 8
        for d in range(2):

            @pl.when(p == 5 + d)
            def _(d=d):
                rows = halves[d]
                csend(k, g, d, 0).wait_recv()
                tb[k, d, rows] = tb[k, d, rows] + rC[k, g, d, 0]
                csend(k, g, d, 2).start()

    corr_one = 1.0 - beta_one**INNER_STEP
    corr_two = 1.0 - beta_two**INNER_STEP

    def stage4(k, t):
        g, p = t // 8, t % 8

        @pl.when(p == 7)
        def _():
            @pl.when(g == 0)
            def _():
                if k == 0:
                    for copy in rest:
                        copy.wait()

            for d in range(2):
                for kind in (1, 2):
                    csend(k, g, d, kind).wait_recv()

            @pl.when(g >= 1)
            def _():
                esend(k, g).wait_send()

            for b in (1 - co, co):
                cols = columns(k, g, b)
                lanes = pl.ds(pl.multiple_of(128 * b, 128), 128)
                for q in range(2):
                    rows = halves[q]
                    grad = (
                        tf[k, rows, lanes]
                        + rC[k, g, 0, 2 - q, :, lanes].astype(F32)
                        + rC[k, g, 1, 1 + q, :, lanes].astype(F32)
                    )
                    here = par[rows, cols]
                    first = beta_one * mom[rows, cols] + (1.0 - beta_one) * grad
                    second = beta_two * var[rows, cols] + (1.0 - beta_two) * grad * grad
                    mom[rows, cols] = first
                    var[rows, cols] = second
                    update = first / corr_one / (jnp.sqrt(second / corr_two) + adam_eps)
                    stepped = here - inner_rate * (update + decay_rate * here)
                    st[k, b, rows] = stepped.astype(BF16)
                    par[rows, cols] = stepped

                if b is not co:
                    esend(k, g).start()

    def stage5(k, t):
        g, p = t // 8, t % 8

        @pl.when(p == 7)
        def _():
            esend(k, g).wait_recv()

            @pl.when(yh != k)
            def _():
                @pl.when(g >= 1)
                def _():
                    psend(k, g).wait_send()

                for rows in halves:
                    ps[rows] = (par[rows, columns(k, g, co)] + rE[k, g, 0, rows].astype(F32)).astype(BF16)
                psend(k, g).start()

    def stage6(k, t):
        g, p = t // 8, t % 8

        @pl.when(jnp.logical_and(p == 7, yh == k))
        def _():
            psend(k, g).wait_recv()
            local = pl.ds(pl.multiple_of(128 * g, 128), 128)
            for rows in halves:
                total = par[rows, columns(k, g, co)] + rE[k, g, 0, rows].astype(F32) + rE[k, g, 1, rows].astype(F32)
                here = anc[rows, local]
                pseudo = here - total / 4.0
                moved = outer_beta * om[rows, local] + pseudo
                om[rows, local] = moved
                nbuf[g, rows] = (here - outer_rate * (pseudo + outer_beta * moved)).astype(BF16)
            for n in (1, 0):
                nsend(g, n).start()
            o_par[:, param_columns(isl, g)] = nbuf[g]

    def stage7(k, t):
        g, p = t // 8, t % 8

        @pl.when(jnp.logical_and(p == 7, yh != k))
        def _():
            relay(g).wait_recv()
            relay(g).start()

    def step(t, _):
        @pl.when(jnp.logical_and(t >= 1, t < 5))
        def _():
            transpose_chunk(t + 3)

        @pl.when(t == 8)
        def _():
            for copy in rest:
                copy.start()

        for delay, stage in ((0, stage0), (D1, stage1), (D2, stage2), (D3, stage3), (D4, stage4), (D5, stage5), (D6, stage6), (D7, stage7)):
            for k in range(2):
                tau = t - delay

                @pl.when(jnp.logical_and(tau >= 0, tau < STEPS))
                def _(tau=tau, k=k, stage=stage):
                    stage(k, tau)

        return 0

    transpose_chunk(0)
    gload.wait()
    pl.semaphore_wait(bar, len(peers))
    stage0(0, jnp.int32(0))

    def before(j):
        if j >= 1:
            transpose_chunk(j)

    stage0(1, jnp.int32(0), before)
    lax.fori_loop(1, STEPS + D7, step, 0)

    for k in range(2):
        for p in range(8):
            for d in range(2):
                for kind in range(3):
                    ring_send(k, p, 0, d, kind, (p < 4, EARLY[p % 4 // 2])).wait_send()
        for p in range(4):
            yearly(k, 0, p, EARLY[p // 2]).wait_send()
            ysend(k, 0, p, EARLY[p // 2]).wait_send()
        for d in range(2):
            for kind in range(3):
                csend(k, 0, d, kind).wait_send()
        esend(k, 0).wait_send()
    psend(0, 0).wait_send()
    for g in range(GROUPS):
        for n in range(2):
            nsend(g, n).wait_send()
        relay(g).wait_send()
        for owner in (2 * yh + 1 - co, 2 * (1 - yh) + 1 - co):
            remote(nbuf.at[g], o_par.at[:, param_columns(owner, g)], sN.at[g, 0], qN.at[owner, g], partner).wait_recv()


PIECES = 2


def hand_on(*refs):
    sources, targets, sems = refs[:4], refs[4:8], refs[8]
    copies = []
    for n, (src, dst) in enumerate(zip(sources, targets)):
        for m in range(PIECES):
            rows = pl.ds(m * (ROWS // PIECES), ROWS // PIECES)
            to = dst.at[0, rows] if len(dst.shape) == 3 else dst.at[rows]
            copies.append(pltpu.make_async_copy(src.at[rows], to, sems.at[n, m]))
    for copy in copies:
        copy.start()
    for copy in copies:
        copy.wait()


def on_device(hidden, grad_out, inner_params, first_moment, second_moment, anchor, outer_momentum):
    dma = pltpu.SemaphoreType.DMA
    vm = pltpu.VMEM
    tile, half, narrow = (ROWS, WIDE), (HALF, WIDE), (ROWS, 128)
    any_spec = pl.BlockSpec(memory_space=pl.ANY)
    shapes = (
        jax.ShapeDtypeStruct((ROWS, D), BF16),
        jax.ShapeDtypeStruct((ROWS, 512), F32),
        jax.ShapeDtypeStruct((1, ROWS, D), F32),
        jax.ShapeDtypeStruct((1, ROWS, D), F32),
    )
    results = pl.pallas_call(
        kernel,
        name="window",
        out_shape=tuple(vm(shape.shape[-2:], shape.dtype) for shape in shapes),
        in_specs=[any_spec] * 7,
        out_specs=(pl.BlockSpec(memory_space=pltpu.VMEM),) * 4,
        scratch_shapes=[
            vm((2, TOK, QROWS), BF16),
            vm((FF, TOK), BF16),
            vm((TOK, D), BF16),
            vm((ROWS, D), F32),
            vm((ROWS, 512), F32),
            vm((2, 8, 4) + tile, BF16),
            vm((2, 4, 4, max(EARLY), WIDE), BF16),
            vm((2, 4, ROWS - min(EARLY), WIDE), BF16),
            vm((2,) + tile, BF16),
            vm((2, 2) + tile, BF16),
            vm((2,) + tile, F32),
            vm((2, 2) + narrow, BF16),
            vm(narrow, BF16),
            vm((GROUPS,) + narrow, BF16),
            vm((2, SLOTS, 2, 3) + half, BF16),
            vm((2, GROUPS, 4, 4, max(EARLY), WIDE), BF16),
            vm((2, GROUPS, 4, ROWS - min(EARLY), WIDE), BF16),
            vm((2, GROUPS, 2, 3) + half, BF16),
            vm((2, GROUPS, 2) + narrow, BF16),
            dma((6,)),
            dma((2,)),
            dma((2, 8, 2, 3)),
            dma((2, 4)),
            dma((2, 4)),
            dma((2, 2, 3)),
            dma((2,)),
            dma,
            dma((GROUPS, 2)),
            dma((GROUPS,)),
            dma((2, SLOTS, 2, 3)),
            dma((2, GROUPS, 4)),
            dma((2, GROUPS, 4)),
            dma((2, GROUPS, 2, 3)),
            dma((2, GROUPS, 2)),
            dma((4, GROUPS)),
        ],
        compiler_params=pltpu.CompilerParams(
            collective_id=0, has_side_effects=True, vmem_limit_bytes=54 * 1024 * 1024
        ),
        cost_estimate=pl.CostEstimate(flops=2 * TOK * FF * D, bytes_accessed=32 << 20, transcendentals=0),
    )(hidden, grad_out, inner_params, first_moment, second_moment, anchor, outer_momentum)
    return pl.pallas_call(
        hand_on,
        name="hand_on",
        out_shape=shapes,
        in_specs=[pl.BlockSpec(memory_space=pltpu.VMEM)] * 4,
        out_specs=(any_spec,) * 4,
        scratch_shapes=[dma((4, PIECES))],
        compiler_params=pltpu.CompilerParams(vmem_limit_bytes=1024 * 1024),
    )(*(pltpu.with_memory_space_constraint(result, pltpu.VMEM) for result in results))


def solution(mesh):
    placed = (
        P("island", "fsdp", None),
        P("island", "fsdp", None),
        P("island", "fsdp", None),
        P("island", "fsdp", None),
        P("island", "fsdp", None),
        P("fsdp", "island"),
        P("fsdp", "island"),
    )
    return jax.shard_map(
        on_device,
        mesh=mesh,
        in_specs=placed,
        out_specs=(
            P("fsdp", None),
            P("fsdp", "island"),
            P("island", "fsdp", None),
            P("island", "fsdp", None),
        ),
        check_vma=False,
    )
```

time: 164 us -> 160 us (0.976)
  Pallas kernels: 163 us -> 159 us
    pallas_call x2, Pallas kernels: 163 us -> 159 us  [the longest x1 157 us: on_device(): pl.pallas_call(kernel, name='window', out_shape=tuple((vm(shape.shape[-2:...]
where the time goes in v2:
time: 160 us
  Pallas kernels  159 us (99%)
    pallas_call x1, Pallas kernels, on_device(): pl.pallas_call(kernel, name='window', out_shape=tuple((vm(shape.shape[-2:...  157 us

profile of v2, /device:TPU:1, one launch (start us, length us, event | category | flops | bytes accessed | tf_op | source)
XLA Modules:
  0.0 159.8 jit_solution(10274001046385343270)
XLA Ops:
  0.6 156.8 %window.1 = (bf16[224,2048]{1,0:T(8,128)(2,1)S(1)}, f32[224,512]{1,0:T(8,128)S(1)}, f32[224,2048]{1,0:T(8,128)S(1)}, f32[224,2048]{1,0:T(8,128)S(1)}) custom-call(bf16[1,768,7168]{2,1,0:T(8,128)(2,1)} %hid.1, bf16[1,768,2048]{2,1,0:T(8,128)(2,1)} %gra.1, f32[1,224,2048]{2,1,0:T(8,128)} %par_h.1, f32[1,224,2048]{2,1,0:T(8,128)} %mom_h.1, ...), custom_call_target="tpu_custom_call" | custom-call | flops 22548578304 | bytes 33554432 | tf_op jit(solution)/shard_map/window/pallas_call | solution.py:474
  157.5 2.4 %hand_on.1 = (bf16[224,2048]{1,0:T(8,128)(2,1)}, f32[224,512]{1,0:T(8,128)}, f32[1,224,2048]{2,1,0:T(8,128)}, f32[1,224,2048]{2,1,0:T(8,128)}) custom-call(bf16[224,2048]{1,0:T(8,128)(2,1)S(1)} %get-tuple-element.8.refs_0_, f32[224,512]{1,0:T(8,128)S(1)} %get-tuple-element.9.refs_1_, f32[224,2048]{1,0:T(8,128)S(1)} %get-tuple-element.10.refs_2_, ...), custom_call_target="tpu_custom_call" | custom-call | tf_op jit(solution)/shard_map/hand_on/pallas_call | solution.py:522
